TPU v7x, 512 devices: a whole 4x8x8 slice. The times are simulated.
512 devices in a mesh: dom: 32 (over y, x), grp: 16 (over z, core).
Axes of the slice: x: 4, y: 8, z: 8, core: 2. Of those that a mesh axis runs over, the one named last changes fastest.
Arguments:
- features: float32 [262144, 128], P(('dom', 'grp')), may hold values from -6 to 6
- w_self: float32 [128, 128], replicated, may hold values from -0.5 to 0.5
- w_neigh: float32 [128, 128], replicated, may hold values from -0.5 to 0.5
- bias: float32 [128], replicated, may hold values from -3 to 3
- cotangent: float32 [262144, 128], P(('dom', 'grp')), may hold values from -6 to 6
- neighbours: int32 [10, 262144], P(None, ('dom', 'grp')), may hold values from 0 to 1279
- degree: int32 [262144], P(('dom', 'grp')), may hold values from 1 to 10
- halo_rows: int32 [65536], P(('dom', 'grp')), may hold values from 0 to 511
- send_rows: int32 [32, 16, 32, 16], P('dom', 'grp'), may hold values from 0 to 511
Outputs:
- activated: float32 [262144, 128], P(('dom', 'grp'))
- grad_features: float32 [262144, 128], P(('dom', 'grp'))
- grad_w_self: float32 [128, 128], replicated
- grad_w_neigh: float32 [128, 128], replicated
- grad_bias: float32 [128], replicated
Inputs may be any that keep to these rules, and one draw needn't show every extreme that they name: `neighbours`: A row of the source table of the vertex's own device; slots s >= degree hold a row too and are ignored. `halo_rows`: local row numbers; a row may be listed more than once. `send_rows`: local row numbers of the sending device; a row may be listed more than once.
All inputs are finite; a program needn't handle non-finite values.
Results may differ from a plain program's by a relative error of at most 0.00008.
Values sent between devices are 32-bit elements; how exact they have to be, the bound alone decides.
A program may use at most 64 MiB of HBM per device.

v0:
```python
import jax
import jax.numpy as jnp
from jax import lax
from jax.sharding import PartitionSpec as P


def extended_2(cells, sides, width):
    for axis, dim in sides:
        count = lax.axis_size(axis)
        head = lax.slice_in_dim(cells, 0, width, axis=dim)
        tail = lax.slice_in_dim(cells, cells.shape[dim] - width, cells.shape[dim], axis=dim)
        cells = jnp.concatenate(
            [
                lax.ppermute(tail, axis, [(i, (i + 1) % count) for i in range(count)]),
                cells,
                lax.ppermute(head, axis, [((i + 1) % count, i) for i in range(count)]),
            ],
            axis=dim,
        )
    return cells


def from_behind(array, axis, by):
    count = lax.axis_size(axis)
    return lax.ppermute(array, axis, [(i, (i + by) % count) for i in range(count)])


def count_matrix(slot_block, live_block, width):
    columns = jnp.arange(width, dtype=jnp.int32)
    counts = jnp.zeros((slot_block.shape[1], width), jnp.float32)
    for step in range(slot_block.shape[0]):
        match = (slot_block[step][:, None] == columns[None, :]).astype(jnp.float32)
        counts = counts + match * live_block[step][:, None]
    return counts


def shards(features, w_self, w_neigh, bias, cotangent, neighbours, degree, halo_rows, send_rows):
    highest = lax.Precision.HIGHEST
    node_count = features.shape[0]
    halo_count = halo_rows.shape[0]
    partitions = lax.axis_size("dom")
    send_count = send_rows.shape[3]
    slot_count = neighbours.shape[0]
    row_width = features.shape[1]
    table_rows = node_count + 2 * halo_count + partitions * send_count
    block_rows = min(512, node_count)
    block_count = node_count // block_rows
    send_index = send_rows.reshape(partitions * send_count)
    live_mask = (jnp.arange(slot_count, dtype=jnp.int32)[:, None] < degree[None, :]).astype(
        jnp.float32
    )
    inverse_degree = 1.0 / degree.astype(jnp.float32)
    slot_blocks = jnp.transpose(neighbours.reshape(slot_count, block_count, block_rows), (1, 0, 2))
    live_blocks = jnp.transpose(live_mask.reshape(slot_count, block_count, block_rows), (1, 0, 2))
    shared = features[halo_rows]
    extended = extended_2(shared, (("grp", 0),), halo_count)
    outgoing = features[send_index].reshape(partitions, send_count, row_width)
    incoming = lax.all_to_all(outgoing, "dom", split_axis=0, concat_axis=0, tiled=True)
    remote_table = jnp.concatenate(
        [
            extended[:halo_count],
            extended[2 * halo_count :],
            incoming.reshape(partitions * send_count, row_width),
        ],
        axis=0,
    )
    source_table = jnp.concatenate([features, remote_table], axis=0)

    def table_block(pair):
        counts = count_matrix(pair[0], pair[1], table_rows)
        return jnp.dot(counts, source_table, precision=highest, preferred_element_type=jnp.float32)

    summed = lax.map(table_block, (slot_blocks, live_blocks)).reshape(node_count, row_width)
    aggregate = summed * inverse_degree[:, None]
    pre = jnp.dot(features, w_self, precision=highest, preferred_element_type=jnp.float32) + bias
    pre = pre + jnp.dot(aggregate, w_neigh, precision=highest, preferred_element_type=jnp.float32)
    activated, gelu_pull = jax.vjp(lambda value: jax.nn.gelu(value, approximate=True), pre)
    (pre_grad,) = gelu_pull(cotangent)
    target_grad = jnp.dot(
        pre_grad, w_neigh.T, precision=highest, preferred_element_type=jnp.float32
    )
    edge_grad = (target_grad * inverse_degree[:, None]).reshape(block_count, block_rows, row_width)

    def spread_block(carry, triple):
        counts = count_matrix(triple[0], triple[1], table_rows)
        term = lax.dot_general(
            counts,
            triple[2],
            (((0,), (0,)), ((), ())),
            precision=highest,
            preferred_element_type=jnp.float32,
        )
        return (carry + term, None)

    table_grad, unused = lax.scan(
        spread_block,
        jnp.zeros((table_rows, row_width), jnp.float32),
        (slot_blocks, live_blocks, edge_grad),
    )
    lower_grad = table_grad[node_count : node_count + halo_count]
    upper_grad = table_grad[node_count + halo_count : node_count + 2 * halo_count]
    boundary_grad = table_grad[node_count + 2 * halo_count :].reshape(
        partitions, send_count, row_width
    )
    returned = lax.all_to_all(boundary_grad, "dom", split_axis=0, concat_axis=0, tiled=True)
    from_upper = from_behind(lower_grad, "grp", -1)
    from_lower = from_behind(upper_grad, "grp", 1)
    shared_grad = from_upper + from_lower
    extra_rows = jnp.concatenate([halo_rows, send_index])
    extra_values = jnp.concatenate(
        [shared_grad, returned.reshape(partitions * send_count, row_width)], axis=0
    )
    placement_table = (
        jnp.arange(node_count, dtype=jnp.int32)[:, None] == extra_rows[None, :]
    ).astype(jnp.float32)
    local_grad = table_grad[:node_count] + jnp.dot(
        placement_table, extra_values, precision=highest, preferred_element_type=jnp.float32
    )
    grad_features = (
        jnp.dot(pre_grad, w_self.T, precision=highest, preferred_element_type=jnp.float32)
        + local_grad
    )
    grad_ws = jnp.dot(features.T, pre_grad, precision=highest, preferred_element_type=jnp.float32)
    grad_wn = jnp.dot(aggregate.T, pre_grad, precision=highest, preferred_element_type=jnp.float32)
    grad_b = jnp.sum(pre_grad, axis=0)
    total_ws, total_wn, total_b = lax.psum((grad_ws, grad_wn, grad_b), ("dom", "grp"))
    scale = 1.0 / jnp.sqrt(jnp.float32(node_count * lax.axis_size("dom") * lax.axis_size("grp")))
    return (activated, grad_features, total_ws * scale, total_wn * scale, total_b * scale)


def solution(mesh):
    placed = (
        P(("dom", "grp"), None),
        P(),
        P(),
        P(),
        P(("dom", "grp"), None),
        P(None, ("dom", "grp")),
        P(("dom", "grp")),
        P(("dom", "grp")),
        P("dom", "grp", None, None),
    )
    return jax.shard_map(
        shards,
        mesh=mesh,
        in_specs=placed,
        out_specs=(P(("dom", "grp"), None), P(("dom", "grp"), None), P(), P(), P()),
        check_vma=False,
    )
```

profile of v0, /device:TPU:1, one launch (start us, length us, event | category | flops | bytes accessed | tf_op | source)
XLA Modules:
  0.0 344.9 jit_solution(18022115102993638895)
XLA Ops:
  7.2 0.7 compare_select_fusion.1
  7.9 1.6 gather_fusion
  9.5 3.5 %collective-permute-start = (f32[128,128]{1,0:T(8,128)S(1)}, f32[128,128]{1,0:T(8,128)S(1)}, u32[]{:S(2)}, u32[]{:S(2)}) collective-permute-start(f32[128,128]{1,0:T(8,128)S(1)} %gather_fusion), channel_id=1, source_target_pairs={{0,1},{1,2},{2,3},{3,4},{4,5},{5,6},{6,7},{7,8},{8,9},{9,10},{10,1... | collective-permute-start | bytes 196616 | tf_op jit(solution)/shard_map/ppermute | solution.py:14
  13.0 3.4 collective-permute-start.1
  16.4 0.8 copy.17
  17.3 1.6 gather_fusion.1
  19.0 6.4 %all-to-all-start = ((f32[32,16,128]{2,1,0:T(8,128)}), f32[32,16,128]{2,1,0:T(8,128)S(1)}, u32[]{:S(2)}, u32[]{:S(2)}) async-start(f32[32,16,128]{2,1,0:T(8,128)} %bitcast.21), calls=%async_computation | async-start | bytes 524288 | tf_op jit(solution)/shard_map/all_to_all | solution.py:58
  26.0 9.8 %all-to-all-done = f32[32,16,128]{2,1,0:T(8,128)S(1)} async-done(((f32[32,16,128]{2,1,0:T(8,128)}), f32[32,16,128]{2,1,0:T(8,128)S(1)}, u32[]{:S(2)}, u32[]{:S(2)}) %all-to-all-start) | async-done | bytes 262176 | tf_op jit(solution)/shard_map/all_to_all | solution.py:58
  35.8 5.5 %convolution_multiply_fusion.1 = f32[512,128]{1,0:T(8,128)S(1)} fusion(f32[512,128]{1,0:T(8,128)S(1)} %bitcast.45, f32[128,128]{1,0:T(8,128)S(1)} %collective-permute-done.1, f32[128,128]{1,0:T(8,128)S(1)} %collective-permute-done, f32[512,128]{1,0:T(8,128)S(1)} %copy-done.1, f32[512]{0:T(512)S(1)} %bitcast.69, s32[512]{0:T(512)S(1)} %bitcast.63, ...), kind=kOutput, calls=%fused_computation.20 | convolution fusion | flops 1026195456 | bytes 960512 | tf_op jit(solution)/shard_map/while/body/eval_jaxpr/dot_general | solution.py:71
  41.3 1.2 fusion.26
  42.5 1.2 fusion.32
  43.7 1.2 convolution_bitcast_fusion
  45.7 7.6 %fusion.11 = f32[1280,128]{1,0:T(8,128)S(1)} fusion(f32[512,128]{1,0:T(8,128)S(1)} %convolution_multiply_fusion, f32[512]{0:T(512)S(1)} %bitcast.70, s32[512]{0:T(512)S(1)} %bitcast.64, f32[512]{0:T(512)S(1)} %bitcast.72, s32[512]{0:T(512)S(1)} %bitcast.66, f32[512]{0:T(512)S(1)} %bitcast.74, s32[512]{0:T(512)S(1)} %bitcast.50, f32[512]{0:T(512)S(1)} %bitcast.76, ...), kind=kOutput, calls=%fused_computation.30 | convolution fusion | flops 1025638400 | bytes 958464 | tf_op jit(solution)/shard_map/while/body/eval_jaxpr/dot_general | solution.py:86
  53.4 0.7 slice.175
  54.1 3.9 %all-to-all-start.1 = ((f32[32,16,128]{2,1,0:T(8,128)}), f32[32,16,128]{2,1,0:T(8,128)S(1)}, u32[]{:S(2)}, u32[]{:S(2)}) async-start(f32[32,16,128]{2,1,0:T(8,128)} %bitcast.23), calls=%async_computation.1 | async-start | bytes 524288 | tf_op jit(solution)/shard_map/all_to_all | solution.py:105
  58.0 0.7 all-reduce.3.cloned.1.call-update
  58.7 105.7 %psum.23 = f32[128]{0:T(128)S(1)} all-reduce(f32[128]{0:T(128)S(1)} %get-tuple-element.47), channel_id=1, replica_groups=mesh['dom'=32,'grp'=16] {'dom','grp'}, use_global_device_ids=true, to_apply=%region_3.4 | all-reduce | flops 128 | bytes 1024 | tf_op jit(solution)/shard_map/psum | solution.py:126
  164.4 0.5 broadcast_multiply_fusion.2
  164.9 1.3 collective-permute-start.3
  166.2 168.0 %all-reduce.3.cloned.1.call-done = (f32[128,128]{0,1:T(8,128)}, f32[128,128]{0,1:T(8,128)}) async-done(((f32[128,128]{0,1:T(8,128)}, f32[128,128]{0,1:T(8,128)}), (f32[128,128]{0,1:T(8,128)}, f32[128,128]{0,1:T(8,128)})) %all-reduce.3.cloned.1.call-update) | async-done | bytes 131088 | tf_op jit(solution)/shard_map/psum | solution.py:126
  334.3 0.9 broadcast_multiply_fusion
  335.1 0.7 copy.21
  335.9 0.7 copy.20
  336.6 1.4 fusion.2
  (38 shorter events, 1.5 us)
Async XLA Ops:
  7.2 34.1 %copy-start = (f32[128,128]{1,0:T(8,128)S(1)}, f32[128,128]{1,0:T(8,128)}, u32[]{:S(2)}) copy-start(f32[128,128]{1,0:T(8,128)} %param.11) | copy-start | bytes 196612
  7.2 10.1 %copy-start.1 = (f32[512,128]{1,0:T(8,128)S(1)}, f32[512,128]{1,0:T(8,128)}, u32[]{:S(2)}) copy-start(f32[512,128]{1,0:T(8,128)} %param.9) | copy-start | bytes 786436
  9.5 16.5 %collective-permute-start = (f32[128,128]{1,0:T(8,128)S(1)}, f32[128,128]{1,0:T(8,128)S(1)}, u32[]{:S(2)}, u32[]{:S(2)}) collective-permute-start(f32[128,128]{1,0:T(8,128)S(1)} %gather_fusion), channel_id=1, source_target_pairs={{0,1},{1,2},{2,3},{3,4},{4,5},{5,6},{6,7},{7,8},{8,9},{9,10},{10,1... | collective-permute-start | bytes 196616 | tf_op jit(solution)/shard_map/ppermute | solution.py:14
  13.0 13.0 %collective-permute-start.1 = (f32[128,128]{1,0:T(8,128)S(1)}, f32[128,128]{1,0:T(8,128)S(1)}, u32[]{:S(2)}, u32[]{:S(2)}) collective-permute-start(f32[128,128]{1,0:T(8,128)S(1)} %gather_fusion), channel_id=1, source_target_pairs={{1,0},{2,1},{3,2},{4,3},{5,4},{6,5},{7,6},{8,7},{9,8},{10,9},{11,1... | collective-permute-start | bytes 196616 | tf_op jit(solution)/shard_map/ppermute | solution.py:16
  17.3 8.2 %copy-start.3 = (s32[10,512]{1,0:T(8,128)S(1)}, s32[10,512]{1,0:T(8,128)}, u32[]{:S(2)}) copy-start(s32[10,512]{1,0:T(8,128)} %param.14) | copy-start | bytes 61444
  17.3 8.2 %copy-start.4 = (s32[512]{0:T(512)S(1)}, s32[512]{0:T(512)}, u32[]{:S(2)}) copy-start(s32[512]{0:T(512)} %param.15) | copy-start | bytes 6148
  19.0 6.6 %copy-start.2 = (f32[128,128]{1,0:T(8,128)S(1)}, f32[128,128]{1,0:T(8,128)}, u32[]{:S(2)}) copy-start(f32[128,128]{1,0:T(8,128)} %param.10) | copy-start | bytes 196612
  19.0 6.6 %copy-start.6 = (f32[128]{0:T(128)S(1)}, f32[128]{0:T(128)}, u32[]{:S(2)}) copy-start(f32[128]{0:T(128)} %param.12) | copy-start | bytes 1540
  19.0 7.0 %copy-start.5 = (s32[128]{0:T(128)S(1)}, s32[128]{0:T(128)}, u32[]{:S(2)}) copy-start(s32[128]{0:T(128)} %param.16) | copy-start | bytes 1540
  19.0 16.8 %all-to-all-start = ((f32[32,16,128]{2,1,0:T(8,128)}), f32[32,16,128]{2,1,0:T(8,128)S(1)}, u32[]{:S(2)}, u32[]{:S(2)}) async-start(f32[32,16,128]{2,1,0:T(8,128)} %bitcast.21), calls=%async_computation | async-start | bytes 524288 | tf_op jit(solution)/shard_map/all_to_all | solution.py:58
  35.8 5.5 %copy-start.7 = (f32[512,128]{1,0:T(8,128)S(1)}, f32[512,128]{1,0:T(8,128)}, u32[]{:S(2)}) copy-start(f32[512,128]{1,0:T(8,128)} %param.13) | copy-start | bytes 786436
  54.1 282.5 %all-to-all-start.1 = ((f32[32,16,128]{2,1,0:T(8,128)}), f32[32,16,128]{2,1,0:T(8,128)S(1)}, u32[]{:S(2)}, u32[]{:S(2)}) async-start(f32[32,16,128]{2,1,0:T(8,128)} %bitcast.23), calls=%async_computation.1 | async-start | bytes 524288 | tf_op jit(solution)/shard_map/all_to_all | solution.py:105
  58.0 276.3 %all-reduce.3.cloned.1.call-start = ((), (), s32[]{:S(2)}) async-start(), calls=%async_computation.2 | async-start | bytes 262144 | tf_op jit(solution)/shard_map/psum | solution.py:126
  164.9 171.7 %collective-permute-start.3 = (f32[128,128]{1,0:T(8,128)S(1)}, f32[128,128]{1,0:T(8,128)S(1)}, u32[]{:S(2)}, u32[]{:S(2)}) collective-permute-start(f32[128,128]{1,0:T(8,128)S(1)} %get-tuple-element.49), channel_id=1, source_target_pairs={{0,1},{1,2},{2,3},{3,4},{4,5},{5,6},{6,7},{7,8},{8,9},{9,10},{10,1... | collective-permute-start | bytes 196616 | tf_op jit(solution)/shard_map/ppermute | solution.py:25
  166.2 170.4 %collective-permute-start.2 = (f32[128,128]{1,0:T(8,128)S(1)}, f32[128,128]{1,0:T(8,128)S(1)}, u32[]{:S(2)}, u32[]{:S(2)}) collective-permute-start(f32[128,128]{1,0:T(8,128)S(1)} %get-tuple-element.50), channel_id=1, source_target_pairs={{0,15},{1,0},{2,1},{3,2},{4,3},{5,4},{6,5},{7,6},{8,7},{9,8},{10,9... | collective-permute-start | bytes 196616 | tf_op jit(solution)/shard_map/ppermute | solution.py:25
Sparse Core Ops, SparseCore 0:
  64.6 269.6 all-reduce.2
where the time goes:
time: 345 us
  waiting for transfers between devices  178 us (52%)
  blocking collectives  106 us (31%)
  matrix products  19.3 us (6%)
  starting transfers between devices  18.5 us (5%)
  between operations  14.3 us (4%)
  local copies, waits for them, and re-layouts  6.44 us (2%)
    psum x1, waiting for transfers between devices, shards(): lax.psum((grad_ws, grad_wn, grad_b), ('dom', 'grp'))  168 us
    psum x1, blocking collectives, shards(): lax.psum((grad_ws, grad_wn, grad_b), ('dom', 'grp'))  106 us
    all_to_all x1, waiting for transfers between devices, shards(): lax.all_to_all(outgoing, 'dom', split_axis=0, concat_axis=0, tiled=True)  9.8 us
    dot_general x1, matrix products, spread_block(): lax.dot_general(counts, triple[2], (((0,), (0,)), ((), ())), precision=hi...  7.62 us
  transfers between devices with their start and end apart: 7, of which 2 were waited for; matrix products, arithmetic and copies ran while one was open for 2% of the time, Pallas kernels for 0%

commit v1 on v0

v1 whole, which is shorter than its diff:
```python
import functools

import jax
import jax.numpy as jnp
from jax import lax
from jax.experimental import pallas as pl
from jax.experimental.pallas import tpu as pltpu
from jax.sharding import PartitionSpec as P

MESH = pl.DeviceIdType.MESH
F32 = jnp.float32
BF16 = jnp.bfloat16


def halves(value):
    high = value.astype(BF16)
    low = (value - high.astype(F32)).astype(BF16)
    return high, low


def stacked(value):
    return jnp.concatenate(halves(value), axis=0)


def beside(value):
    return jnp.concatenate(halves(value), axis=1)


def folded_rows(product):
    count = product.shape[0] // 2
    return product[:count] + product[count:]


def folded_columns(product):
    count = product.shape[1] // 2
    return product[:, :count] + product[:, count:]


def weight_pair(weight):
    high, low = halves(weight)
    return jnp.concatenate(
        [jnp.concatenate([high, high], axis=1), jnp.concatenate([low, low], axis=1)], axis=0
    )


def matmul(left, right):
    return jnp.dot(left, right, preferred_element_type=F32)


def matmul_nt(left, right):
    return lax.dot_general(left, right, (((1,), (1,)), ((), ())), preferred_element_type=F32)


def kernel(
    partitions,
    groups,
    width_x,
    scale,
    features_hbm,
    w_self_hbm,
    w_neigh_hbm,
    bias_hbm,
    cotangent_hbm,
    neighbours_hbm,
    degree_hbm,
    halo_hbm,
    send_hbm,
    activated_hbm,
    grad_features_hbm,
    grad_ws_hbm,
    grad_wn_hbm,
    grad_b_hbm,
    features,
    w_self,
    w_neigh,
    bias,
    cotangent,
    neighbours,
    degree,
    halo,
    send,
    counts,
    placement,
    outgoing,
    table,
    table_grad,
    back,
    activated,
    grad_features,
    weight_grad,
    bias_grad,
    scatter_slots,
    bias_slots,
    x_slots,
    y_slots,
    piece,
    gathered,
    total_b,
    in_sem,
    out_sem,
    send_sem,
    recv_sem,
):
    node_count, feat = features.shape
    halo_count = halo.shape[1]
    send_count = send.shape[1]
    slot_count = neighbours.shape[0]
    remote_rows = table.shape[0]
    table_rows = node_count + remote_rows
    width_y = partitions // width_x
    piece_rows = 2 * feat // groups

    dom = lax.axis_index("dom")
    grp = lax.axis_index("grp")
    at_y = dom // width_x
    at_x = lax.rem(dom, width_x)
    upper = lax.rem(grp + 1, groups)
    lower = lax.rem(grp + groups - 1, groups)

    ins = [
        pltpu.make_async_copy(source, target, in_sem.at[at])
        for at, (source, target) in enumerate(
            [
                (send_hbm, send),
                (halo_hbm, halo),
                (features_hbm, features),
                (neighbours_hbm, neighbours),
                (degree_hbm, degree),
                (w_self_hbm, w_self),
                (w_neigh_hbm, w_neigh),
                (bias_hbm, bias),
                (cotangent_hbm, cotangent),
            ]
        )
    ]
    for copy in ins:
        copy.start()

    barrier = pltpu.get_barrier_semaphore()

    def greet_dom(step, carry):
        peer = lax.rem(dom + step, partitions)
        pl.semaphore_signal(barrier, inc=1, device_id=(peer, grp), device_id_type=MESH)
        return carry

    def greet_grp(step, carry):
        peer = lax.rem(grp + step, groups)
        pl.semaphore_signal(barrier, inc=1, device_id=(dom, peer), device_id_type=MESH)
        return carry

    lax.fori_loop(1, partitions, greet_dom, 0)
    lax.fori_loop(1, groups, greet_grp, 0)

    ins[0].wait()
    ins[1].wait()
    per_tile = feat // send_count
    tiled = jnp.concatenate([send[...]] * per_tile, axis=1)
    lane = lax.broadcasted_iota(jnp.int32, (per_tile, feat), 1)
    row = lax.broadcasted_iota(jnp.int32, (per_tile, feat), 0)
    own = row == lane // send_count
    index_rows = [halo[...]]
    for tile in range(partitions // per_tile):
        block = tiled[tile * per_tile : (tile + 1) * per_tile]
        index_rows.append(jnp.sum(jnp.where(own, block, 0), axis=0, keepdims=True))
    node_row = lax.broadcasted_iota(jnp.int32, (node_count, feat), 0)
    node_lane = lax.broadcasted_iota(jnp.int32, (feat, node_count), 1)
    ins[2].wait()
    feature_pair = beside(features[...])
    for at, index_row in enumerate(index_rows):
        listed = pl.ds(at * feat, feat)
        index_column = jnp.broadcast_to(index_row, (feat, feat)).T[:, :1]
        pick = jnp.where(index_column == node_lane, 1.0, 0.0).astype(BF16)
        outgoing[listed, :] = folded_columns(matmul(pick, feature_pair))
        placement[:, listed] = jnp.where(index_row == node_row, 1.0, 0.0).astype(BF16)

    pl.semaphore_wait(barrier, partitions + groups - 2)

    def to_dom(source, target, sem, peer):
        return pltpu.make_async_remote_copy(
            src_ref=source,
            dst_ref=target,
            send_sem=send_sem.at[sem],
            recv_sem=recv_sem.at[sem],
            device_id=(peer, grp),
            device_id_type=MESH,
        )

    def to_grp(source, target, sem, peer):
        return pltpu.make_async_remote_copy(
            src_ref=source,
            dst_ref=target,
            send_sem=send_sem.at[sem],
            recv_sem=recv_sem.at[sem],
            device_id=(dom, peer),
            device_id_type=MESH,
        )

    def peer_dom(step):
        peer_y = lax.rem(at_y + step // width_x, width_y)
        peer_x = lax.rem(at_x + lax.rem(step, width_x), width_x)
        return peer_y * width_x + peer_x

    def send_forward(step, carry):
        peer = peer_dom(step)
        to_dom(
            outgoing.at[pl.ds(halo_count + peer * send_count, send_count)],
            table.at[pl.ds(2 * halo_count + dom * send_count, send_count)],
            0,
            peer,
        ).start()
        return carry

    shared = outgoing.at[pl.ds(0, halo_count)]
    halo_up = to_grp(shared, table.at[pl.ds(0, halo_count)], 1, upper)
    halo_down = to_grp(shared, table.at[pl.ds(halo_count, halo_count)], 2, lower)
    lax.fori_loop(1, partitions, send_forward, 0)
    halo_up.start()
    halo_down.start()
    table[pl.ds(2 * halo_count + dom * send_count, send_count), :] = outgoing[
        pl.ds(halo_count + dom * send_count, send_count), :
    ]

    ins[3].wait()
    ins[4].wait()
    slot = lax.broadcasted_iota(jnp.int32, (slot_count, node_count), 0)
    live = jnp.where(slot < degree[...], neighbours[...], -1)
    inverse_degree = 1.0 / degree[...].astype(F32)
    block_rows = 16

    def count_block(step, carry):
        base = pl.multiple_of(step * block_rows, block_rows)
        rows = base + lax.broadcasted_iota(jnp.int32, (block_rows, node_count), 0)
        total = jnp.zeros((block_rows, node_count), F32)
        for at in range(slot_count):
            total = total + jnp.where(rows == live[at : at + 1], 1.0, 0.0)
        counts[pl.ds(base, block_rows), :] = total.astype(BF16)
        return carry

    lax.fori_loop(0, table_rows // block_rows, count_block, 0)

    features_t = stacked(features[...].T)
    aggregate = folded_rows(matmul(features_t, counts[pl.ds(0, node_count), :]))
    for copy in ins[5:]:
        copy.wait()
    bias_column = jnp.broadcast_to(bias[...], (feat, feat)).T[:, :1]
    pre = folded_rows(matmul(weight_pair(w_self[...].T), features_t)) + bias_column
    neigh_t = weight_pair(w_neigh[...].T)
    neigh = weight_pair(w_neigh[...])
    cotangent_t = cotangent[...].T

    received = to_dom(
        table.at[pl.ds(0, (partitions - 1) * send_count)],
        table.at[pl.ds(0, (partitions - 1) * send_count)],
        0,
        lax.rem(dom + 1, partitions),
    )
    received.wait_recv()
    halo_up.wait_recv()
    halo_down.wait_recv()

    table_t = stacked(table[...].T)
    aggregate = aggregate + folded_rows(
        matmul(table_t, counts[pl.ds(node_count, remote_rows), :])
    )
    aggregate_t = stacked(aggregate * inverse_degree)
    pre = pre + folded_rows(matmul(neigh_t, aggregate_t))

    root = 0.7978845608028654
    square = pre * pre
    bent = jnp.tanh(root * (pre + 0.044715 * (square * pre)))
    rise = 0.5 * (1.0 + bent)
    slope = rise + 0.5 * pre * (1.0 - bent * bent) * (root * (1.0 + 3.0 * 0.044715 * square))
    pre_grad = stacked(cotangent_t * slope)

    edge_grad = stacked(folded_rows(matmul(neigh, pre_grad)) * inverse_degree)
    table_grad[...] = folded_columns(
        matmul_nt(counts[pl.ds(node_count, remote_rows), :], edge_grad)
    )

    def send_backward(step, carry):
        peer = peer_dom(step)
        to_dom(
            table_grad.at[pl.ds(2 * halo_count + peer * send_count, send_count)],
            back.at[pl.ds(2 * halo_count + dom * send_count, send_count)],
            3,
            peer,
        ).start()
        return carry

    back_down = to_grp(
        table_grad.at[pl.ds(0, halo_count)], back.at[pl.ds(0, halo_count)], 4, lower
    )
    back_up = to_grp(
        table_grad.at[pl.ds(halo_count, halo_count)],
        back.at[pl.ds(halo_count, halo_count)],
        5,
        upper,
    )
    lax.fori_loop(1, partitions, send_backward, 0)
    back_down.start()
    back_up.start()
    back[pl.ds(2 * halo_count + dom * send_count, send_count), :] = table_grad[
        pl.ds(2 * halo_count + dom * send_count, send_count), :
    ]

    product = folded_columns(
        matmul_nt(jnp.concatenate([features_t, aggregate_t], axis=0), pre_grad)
    )
    weight_grad[pl.ds(0, feat), :] = folded_rows(product[: 2 * feat])
    weight_grad[pl.ds(feat, feat), :] = folded_rows(product[2 * feat :])
    ones = jnp.ones((16, node_count), BF16)
    bias_grad[...] = folded_columns(matmul_nt(ones, pre_grad))[:1]

    def send_scatter(step, carry):
        peer = lax.rem(grp + step, groups)
        to_grp(
            weight_grad.at[pl.ds(peer * piece_rows, piece_rows)],
            scatter_slots.at[pl.ds(grp * piece_rows, piece_rows)],
            6,
            peer,
        ).start()
        to_grp(bias_grad, bias_slots.at[grp], 7, peer).start()
        return carry

    lax.fori_loop(1, groups, send_scatter, 0)
    scatter_slots[pl.ds(grp * piece_rows, piece_rows), :] = weight_grad[
        pl.ds(grp * piece_rows, piece_rows), :
    ]
    bias_slots[grp] = bias_grad[...]

    activated[...] = (pre * rise).T
    out_activated = pltpu.make_async_copy(activated, activated_hbm, out_sem.at[0])
    out_activated.start()
    own_grad = folded_columns(matmul_nt(counts[pl.ds(0, node_count), :], edge_grad))
    own_grad = own_grad + folded_rows(matmul(weight_pair(w_self[...]), pre_grad)).T

    scattered = to_grp(
        scatter_slots.at[pl.ds(0, (groups - 1) * piece_rows)],
        scatter_slots.at[pl.ds(0, (groups - 1) * piece_rows)],
        6,
        upper,
    )
    scattered.wait_recv()
    bias_sent = to_grp(
        bias_slots.at[pl.ds(0, groups - 1)], bias_slots.at[pl.ds(0, groups - 1)], 7, upper
    )
    bias_sent.wait_recv()
    total = scatter_slots[pl.ds(0, piece_rows), :]
    total_bias = bias_slots[0]
    for at in range(1, groups):
        total = total + scatter_slots[pl.ds(at * piece_rows, piece_rows), :]
        total_bias = total_bias + bias_slots[at]
    full_rows = piece_rows + 8

    def put_piece(slots, at, value, value_bias):
        slots[at, pl.ds(0, piece_rows), :] = value
        slots[at, pl.ds(piece_rows, 8), :] = jnp.broadcast_to(value_bias, (8, feat))

    put_piece(x_slots, at_x, total, total_bias)

    def send_x(step, carry):
        peer = at_y * width_x + lax.rem(at_x + step, width_x)
        to_dom(x_slots.at[at_x], x_slots.at[at_x], 8, peer).start()
        return carry

    lax.fori_loop(1, width_x, send_x, 0)
    x_sent = to_dom(
        x_slots.at[pl.ds(0, width_x - 1)],
        x_slots.at[pl.ds(0, width_x - 1)],
        8,
        lax.rem(dom + 1, partitions),
    )
    x_sent.wait_recv()
    total = x_slots[0]
    for at in range(1, width_x):
        total = total + x_slots[at]
    y_slots[at_y] = total

    def send_y(step, carry):
        peer = lax.rem(at_y + step, width_y) * width_x + at_x
        to_dom(y_slots.at[at_y], y_slots.at[at_y], 9, peer).start()
        return carry

    lax.fori_loop(1, width_y, send_y, 0)
    y_sent = to_dom(
        y_slots.at[pl.ds(0, width_y - 1)],
        y_slots.at[pl.ds(0, width_y - 1)],
        9,
        lax.rem(dom + 1, partitions),
    )
    y_sent.wait_recv()
    total = y_slots[0]
    for at in range(1, width_y):
        total = total + y_slots[at]
    total = total * scale
    piece[...] = total[:piece_rows]
    total_b[...] = total[piece_rows : piece_rows + 1]
    out_b = pltpu.make_async_copy(total_b, grad_b_hbm, out_sem.at[1])
    out_b.start()

    def send_gather(step, carry):
        peer = lax.rem(grp + step, groups)
        to_grp(piece, gathered.at[pl.ds(grp * piece_rows, piece_rows)], 10, peer).start()
        return carry

    lax.fori_loop(1, groups, send_gather, 0)
    gathered[pl.ds(grp * piece_rows, piece_rows), :] = piece[...]

    returned = to_dom(
        back.at[pl.ds(0, (partitions - 1) * send_count)],
        back.at[pl.ds(0, (partitions - 1) * send_count)],
        3,
        lax.rem(dom + 1, partitions),
    )
    returned.wait_recv()
    back_down.wait_recv()
    back_up.wait_recv()
    extra = jnp.concatenate(
        [
            back[pl.ds(0, halo_count), :] + back[pl.ds(halo_count, halo_count), :],
            back[pl.ds(2 * halo_count, partitions * send_count), :],
        ],
        axis=0,
    )
    grad_features[...] = own_grad + folded_columns(matmul(placement[...], beside(extra)))
    out_features = pltpu.make_async_copy(grad_features, grad_features_hbm, out_sem.at[2])
    out_features.start()

    collected = to_grp(
        gathered.at[pl.ds(0, (groups - 1) * piece_rows)],
        gathered.at[pl.ds(0, (groups - 1) * piece_rows)],
        10,
        upper,
    )
    collected.wait_recv()
    out_ws = pltpu.make_async_copy(gathered.at[pl.ds(0, feat)], grad_ws_hbm, out_sem.at[3])
    out_wn = pltpu.make_async_copy(gathered.at[pl.ds(feat, feat)], grad_wn_hbm, out_sem.at[4])
    out_ws.start()
    out_wn.start()

    for copy in (
        received,
        halo_up,
        halo_down,
        returned,
        back_down,
        back_up,
        scattered,
        bias_sent,
        x_sent,
        y_sent,
        collected,
    ):
        copy.wait_send()
    for copy in (out_activated, out_b, out_features, out_ws, out_wn):
        copy.wait()


def shards(width_x, features, w_self, w_neigh, bias, cotangent, neighbours, degree, halo_rows, send_rows):
    partitions = lax.axis_size("dom")
    groups = lax.axis_size("grp")
    node_count, feat = features.shape
    hidden = w_self.shape[1]
    halo_count = halo_rows.shape[0]
    send_count = send_rows.shape[3]
    slot_count = neighbours.shape[0]
    remote_rows = 2 * halo_count + partitions * send_count
    listed = halo_count + partitions * send_count
    piece_rows = 2 * feat // groups
    width_y = partitions // width_x
    scale = 1.0 / (node_count * partitions * groups) ** 0.5
    anywhere = pl.BlockSpec(memory_space=pl.ANY)
    activated, grad_features, grad_ws, grad_wn, grad_b = pl.pallas_call(
        functools.partial(kernel, partitions, groups, width_x, scale),
        out_shape=(
            jax.ShapeDtypeStruct((node_count, hidden), F32),
            jax.ShapeDtypeStruct((node_count, feat), F32),
            jax.ShapeDtypeStruct((feat, hidden), F32),
            jax.ShapeDtypeStruct((feat, hidden), F32),
            jax.ShapeDtypeStruct((1, hidden), F32),
        ),
        in_specs=[anywhere] * 9,
        out_specs=(anywhere,) * 5,
        scratch_shapes=[
            pltpu.VMEM((node_count, feat), F32),
            pltpu.VMEM((feat, hidden), F32),
            pltpu.VMEM((feat, hidden), F32),
            pltpu.VMEM((1, hidden), F32),
            pltpu.VMEM((node_count, hidden), F32),
            pltpu.VMEM((slot_count, node_count), jnp.int32),
            pltpu.VMEM((1, node_count), jnp.int32),
            pltpu.VMEM((1, halo_count), jnp.int32),
            pltpu.VMEM((partitions, send_count), jnp.int32),
            pltpu.VMEM((node_count + remote_rows, node_count), BF16),
            pltpu.VMEM((node_count, listed), BF16),
            pltpu.VMEM((listed, feat), F32),
            pltpu.VMEM((remote_rows, feat), F32),
            pltpu.VMEM((remote_rows, feat), F32),
            pltpu.VMEM((remote_rows, feat), F32),
            pltpu.VMEM((node_count, hidden), F32),
            pltpu.VMEM((node_count, feat), F32),
            pltpu.VMEM((2 * feat, hidden), F32),
            pltpu.VMEM((1, hidden), F32),
            pltpu.VMEM((2 * feat, hidden), F32),
            pltpu.VMEM((groups, 1, hidden), F32),
            pltpu.VMEM((width_x, piece_rows + 8, hidden), F32),
            pltpu.VMEM((width_y, piece_rows + 8, hidden), F32),
            pltpu.VMEM((piece_rows, hidden), F32),
            pltpu.VMEM((2 * feat, hidden), F32),
            pltpu.VMEM((1, hidden), F32),
            pltpu.SemaphoreType.DMA((9,)),
            pltpu.SemaphoreType.DMA((5,)),
            pltpu.SemaphoreType.DMA((11,)),
            pltpu.SemaphoreType.DMA((11,)),
        ],
        compiler_params=pltpu.CompilerParams(
            collective_id=0, has_side_effects=True, vmem_limit_bytes=32 * 1024 * 1024
        ),
    )(
        features,
        w_self,
        w_neigh,
        bias.reshape(1, hidden),
        cotangent,
        neighbours,
        degree.reshape(1, node_count),
        halo_rows.reshape(1, halo_count),
        send_rows.reshape(partitions, send_count),
    )
    return activated, grad_features, grad_ws, grad_wn, grad_b.reshape(hidden)


def solution(mesh):
    placed = (
        P(("dom", "grp"), None),
        P(),
        P(),
        P(),
        P(("dom", "grp"), None),
        P(None, ("dom", "grp")),
        P(("dom", "grp")),
        P(("dom", "grp")),
        P("dom", "grp", None, None),
    )
    width_x = 4 if mesh.shape["dom"] % 4 == 0 else 1
    return jax.shard_map(
        functools.partial(shards, width_x),
        mesh=mesh,
        in_specs=placed,
        out_specs=(P(("dom", "grp"), None), P(("dom", "grp"), None), P(), P(), P()),
        check_vma=False,
    )
```

time: 345 us -> 59.5 us (0.17)
  waiting for transfers between devices: 178 us -> 0 us
  blocking collectives: 106 us -> 0 us
  Pallas kernels: 0 us -> 49.5 us
  matrix products: 19.3 us -> 0 us
  starting transfers between devices: 18.5 us -> 0 us
  between operations: 14.3 us -> 0.66 us
    psum x1 -> x0, waiting for transfers between devices: 168 us -> none  [shards(): lax.psum((grad_ws, grad_wn, grad_b), ('dom', 'grp'))]
    psum x1 -> x0, blocking collectives: 106 us -> none  [shards(): lax.psum((grad_ws, grad_wn, grad_b), ('dom', 'grp'))]
    pallas_call x0 -> x1, Pallas kernels: none -> 49.5 us  [shards(): pl.pallas_call(functools.partial(kernel, partitions, groups, width_x, sca...]
    dot_general x9 -> x0, matrix products: 19.3 us -> none  [the longest x1 7.62 us: spread_block(): lax.dot_general(counts, triple[2], (((0,), (0,)), ((), ())), precision=hi...]
    all_to_all x2 -> x0, starting transfers between devices: 10.3 us -> none  [the longest x1 6.39 us: shards(): lax.all_to_all(outgoing, 'dom', split_axis=0, concat_axis=0, tiled=True)]
    all_to_all x2 -> x0, waiting for transfers between devices: 9.8 us -> none  [the longest x1 9.8 us: shards(): lax.all_to_all(outgoing, 'dom', split_axis=0, concat_axis=0, tiled=True)]
    ppermute x4 -> x0, starting transfers between devices: 8.21 us -> none  [the longest x1 3.49 us: extended_2(): lax.ppermute(tail, axis, [(i, (i + 1) % count) for i in range(count)])]
    unnamed x19 -> x22, local copies, waits for them, and re-layouts: 2.27 us -> 8.96 us
  transfers between devices with their start and end apart: 7 -> 0, of which waited for: 2 -> 0; matrix products, arithmetic and copies ran while one was open for 2% -> 0% of each run, Pallas kernels for 0% -> 0%
where the time goes in v1:
time: 59.5 us; the launch traced here: 59.1 us
  Pallas kernels  49.5 us (83%)
  local copies, waits for them, and re-layouts  8.96 us (15%)
  between operations  0.66 us (1%)
    pallas_call x1, Pallas kernels, shards(): pl.pallas_call(functools.partial(kernel, partitions, groups, width_x, sca...  49.5 us
    unnamed x22, local copies, waits for them, and re-layouts  8.96 us

profile of v1, /device:TPU:1, one launch (start us, length us, event | category | flops | bytes accessed | tf_op | source)
XLA Modules:
  0.0 59.1 jit_solution(15913999895440373746)
XLA Ops:
  0.6 0.0 copy-start.5
  0.6 0.8 %copy.14 = s32[1,1,32,16]{3,2,1,0:T(8,128)S(1)} copy(s32[1,1,32,16]{2,3,1,0:T(8,128)} %param.17) | data formatting | bytes 4096 | tf_op args[8]
  1.4 0.0 copy-start.6
  1.4 0.0 copy-start.7
  1.4 0.0 copy-done.5
  1.4 0.6 %copy-done.6 = f32[128]{0:T(128)S(1)} copy-done((f32[128]{0:T(128)S(1)}, f32[128]{0:T(128)}, u32[]{:S(2)}) %copy-start.6) | copy-done | bytes 536
  2.1 0.0 copy-done.7
  2.1 0.0 copy-start
  2.1 0.9 %copy-done = f32[512,128]{1,0:T(8,128)S(1)} copy-done((f32[512,128]{1,0:T(8,128)S(1)}, f32[512,128]{1,0:T(8,128)}, u32[]{:S(2)}) %copy-start) | copy-done | bytes 262168
  3.0 0.0 copy-start.1
  3.0 0.9 %copy-done.1 = f32[512,128]{1,0:T(8,128)S(1)} copy-done((f32[512,128]{1,0:T(8,128)S(1)}, f32[512,128]{1,0:T(8,128)}, u32[]{:S(2)}) %copy-start.1) | copy-done | bytes 262168
  4.0 0.0 copy-start.2
  4.0 0.8 %copy-done.2 = f32[128,128]{1,0:T(8,128)S(1)} copy-done((f32[128,128]{1,0:T(8,128)S(1)}, f32[128,128]{1,0:T(8,128)}, u32[]{:S(2)}) %copy-start.2) | copy-done | bytes 65560
  4.8 0.0 copy-start.3
  4.8 0.8 %copy-done.3 = f32[128,128]{1,0:T(8,128)S(1)} copy-done((f32[128,128]{1,0:T(8,128)S(1)}, f32[128,128]{1,0:T(8,128)}, u32[]{:S(2)}) %copy-start.3) | copy-done | bytes 65560
  5.7 0.0 copy-start.4
  5.7 0.8 %copy-done.4 = s32[10,512]{1,0:T(8,128)S(1)} copy-done((s32[10,512]{1,0:T(8,128)S(1)}, s32[10,512]{1,0:T(8,128)}, u32[]{:S(2)}) %copy-start.4) | copy-done | bytes 20504
  6.4 49.5 %shard_map.128 = (f32[512,128]{1,0:T(8,128)S(1)}, f32[512,128]{1,0:T(8,128)S(1)}, f32[128,128]{1,0:T(8,128)S(1)}, f32[128,128]{1,0:T(8,128)S(1)}, f32[1,128]{1,0:T(1,128)S(1)}) custom-call(f32[512,128]{1,0:T(8,128)S(1)} %copy-done, f32[128,128]{1,0:T(8,128)S(1)} %copy-done.2, f32[128,128]{1,0:T(8,128)S(1)} %copy-done.3, f32[1,128]{1,0:T(1,128)S(1)} %bitcast.7, ...), custom_call_target="tpu_custom_call" | custom-call | tf_op jit(solution)/shard_map/pallas_call | solution.py:473
  56.0 0.7 %copy.20 = f32[512,128]{1,0:T(8,128)} copy(f32[512,128]{1,0:T(8,128)S(1)} %get-tuple-element.20) | data formatting | bytes 524288
  56.7 0.7 %copy.21 = f32[512,128]{1,0:T(8,128)} copy(f32[512,128]{1,0:T(8,128)S(1)} %get-tuple-element.21) | data formatting | bytes 524288
  57.4 0.6 %copy.22 = f32[128,128]{1,0:T(8,128)} copy(f32[128,128]{1,0:T(8,128)S(1)} %get-tuple-element.22) | data formatting | bytes 131072
  58.0 0.6 %copy.23 = f32[128,128]{1,0:T(8,128)} copy(f32[128,128]{1,0:T(8,128)S(1)} %get-tuple-element.23) | data formatting | bytes 131072
  58.6 0.5 copy.24
Async XLA Ops:
  0.6 0.8 %copy-start.5 = (s32[512]{0:T(512)S(1)}, s32[512]{0:T(512)}, u32[]{:S(2)}) copy-start(s32[512]{0:T(512)} %param.15) | copy-start | bytes 6148
  1.4 0.7 %copy-start.6 = (f32[128]{0:T(128)S(1)}, f32[128]{0:T(128)}, u32[]{:S(2)}) copy-start(f32[128]{0:T(128)} %param.12) | copy-start | bytes 1540
  1.4 0.7 %copy-start.7 = (s32[128]{0:T(128)S(1)}, s32[128]{0:T(128)}, u32[]{:S(2)}) copy-start(s32[128]{0:T(128)} %param.16) | copy-start | bytes 1540
  2.1 0.9 %copy-start = (f32[512,128]{1,0:T(8,128)S(1)}, f32[512,128]{1,0:T(8,128)}, u32[]{:S(2)}) copy-start(f32[512,128]{1,0:T(8,128)} %features_hbm.1) | copy-start | bytes 786436
  3.0 0.9 %copy-start.1 = (f32[512,128]{1,0:T(8,128)S(1)}, f32[512,128]{1,0:T(8,128)}, u32[]{:S(2)}) copy-start(f32[512,128]{1,0:T(8,128)} %cotangent_hbm.1) | copy-start | bytes 786436
  4.0 0.8 %copy-start.2 = (f32[128,128]{1,0:T(8,128)S(1)}, f32[128,128]{1,0:T(8,128)}, u32[]{:S(2)}) copy-start(f32[128,128]{1,0:T(8,128)} %w_self_hbm.1) | copy-start | bytes 196612
  4.8 0.8 %copy-start.3 = (f32[128,128]{1,0:T(8,128)S(1)}, f32[128,128]{1,0:T(8,128)}, u32[]{:S(2)}) copy-start(f32[128,128]{1,0:T(8,128)} %w_neigh_hbm.1) | copy-start | bytes 196612
  5.7 0.8 %copy-start.4 = (s32[10,512]{1,0:T(8,128)S(1)}, s32[10,512]{1,0:T(8,128)}, u32[]{:S(2)}) copy-start(s32[10,512]{1,0:T(8,128)} %neighbours_hbm.1) | copy-start | bytes 61444

commit v2 on v1

v2 whole, which is shorter than its diff:
```python
import functools

import jax
import jax.numpy as jnp
from jax import lax
from jax.experimental import pallas as pl
from jax.experimental.pallas import tpu as pltpu
from jax.sharding import PartitionSpec as P

MESH = pl.DeviceIdType.MESH
F32 = jnp.float32
BF16 = jnp.bfloat16
WIDTH_X = 4
WIDTH_C = 2


def halves(value):
    high = value.astype(BF16)
    low = (value - high.astype(F32)).astype(BF16)
    return high, low


def stacked(value):
    return jnp.concatenate(halves(value), axis=0)


def beside(value):
    return jnp.concatenate(halves(value), axis=1)


def folded_rows(product):
    count = product.shape[0] // 2
    return product[:count] + product[count:]


def folded_columns(product):
    count = product.shape[1] // 2
    return product[:, :count] + product[:, count:]


def weight_pair(weight):
    high, low = halves(weight)
    return jnp.concatenate(
        [jnp.concatenate([high, high], axis=1), jnp.concatenate([low, low], axis=1)], axis=0
    )


def matmul(left, right):
    return jnp.dot(left, right, preferred_element_type=F32)


def matmul_nt(left, right):
    return lax.dot_general(left, right, (((1,), (1,)), ((), ())), preferred_element_type=F32)


def far_first(count):
    return sorted(range(count), key=lambda at: (-min(at, count - at), at))


def kernel(
    widths,
    scale,
    features_hbm,
    w_self_hbm,
    w_neigh_hbm,
    bias_hbm,
    cotangent_hbm,
    neighbours_hbm,
    degree_hbm,
    halo_hbm,
    send_hbm,
    activated,
    grad_features,
    gathered,
    total_b,
    features,
    w_self,
    w_neigh,
    bias,
    cotangent,
    neighbours,
    degree,
    halo,
    send,
    counts,
    placement,
    outgoing,
    table,
    table_grad,
    back,
    weight_grad,
    zx_slots,
    x_bias,
    yc_slots,
    yc_bias,
    z_bias,
    piece,
    in_sem,
    send_sem,
    recv_sem,
):
    width_y, width_x, width_z, width_c = widths
    partitions = width_y * width_x
    groups = width_z * width_c
    node_count, feat = features.shape
    halo_count = halo.shape[1]
    send_count = send.shape[0]
    slot_count = neighbours.shape[0]
    remote_rows = table.shape[0]
    table_rows = node_count + remote_rows
    pieces = width_z * width_x
    piece_rows = 2 * feat // pieces
    boundary = 2 * halo_count
    steps = [(step_y, step_x) for step_y in far_first(width_y) for step_x in far_first(width_x)]
    steps.remove((0, 0))
    far_steps = partitions // 2
    far_rows = far_steps * send_count
    near_rows = (partitions - 1 - far_steps) * send_count

    dom = lax.axis_index("dom")
    grp = lax.axis_index("grp")
    at_y = dom // width_x
    at_x = lax.rem(dom, width_x)
    at_z = grp // width_c
    at_c = lax.rem(grp, width_c)
    upper = lax.rem(grp + 1, groups)
    lower = lax.rem(grp + groups - 1, groups)

    def ring(at, count):
        places = [at + over for over in range(count)]
        return [jnp.where(place >= count, place - count, place) for place in places]

    over_y, over_x = ring(at_y, width_y), ring(at_x, width_x)
    over_z, over_c = ring(at_z, width_z), ring(at_c, width_c)

    def dom_at(step):
        return over_y[step[0]] * width_x + over_x[step[1]]

    def dom_before(step):
        return over_y[-step[0]] * width_x + over_x[-step[1]]

    def grp_at(step_z, step_c):
        return over_z[step_z] * width_c + over_c[step_c]

    def apart(step, count):
        return min(step, count - step)

    zx_steps = [(step_z, step_x) for step_z in range(width_z) for step_x in range(width_x)][1:]
    zx_steps.sort(key=lambda step: -apart(step[0], width_z) - apart(step[1], width_x))
    zx_peers = [
        (dom_at((0, step[1])), grp_at(step[0], 0), over_z[step[0]] * width_x + over_x[step[1]])
        for step in zx_steps
    ]
    own_zx = at_z * width_x + at_x
    yc_steps = [(step_y, step_c) for step_y in far_first(width_y) for step_c in range(width_c)]
    yc_steps.remove((0, 0))
    yc_peers = [(dom_at((step[0], 0)), grp_at(0, step[1])) for step in yc_steps]
    own_yc = at_y * width_c + at_c

    ins = [
        pltpu.make_async_copy(source, target, in_sem.at[at])
        for at, (source, target) in enumerate(
            [
                (send_hbm, send),
                (halo_hbm, halo),
                (features_hbm, features),
                (neighbours_hbm, neighbours),
                (degree_hbm, degree),
                (w_self_hbm, w_self),
                (w_neigh_hbm, w_neigh),
                (bias_hbm, bias),
                (cotangent_hbm, cotangent),
            ]
        )
    ]
    for copy in ins:
        copy.start()

    barrier = pltpu.get_barrier_semaphore()
    guests = [(dom_at(step), grp) for step in steps]
    guests += [peer[:2] for step, peer in zip(zx_steps, zx_peers) if step[0] != 0]
    guests += [peer for step, peer in zip(yc_steps, yc_peers) if step[1] != 0]
    guests += [(dom, upper), (dom, lower)]
    for guest in guests:
        pl.semaphore_signal(barrier, inc=1, device_id=guest, device_id_type=MESH)

    ins[0].wait()
    ins[1].wait()
    per_tile = feat // send_count
    tiled = jnp.concatenate([send[...].T] * per_tile, axis=1)
    lane = lax.broadcasted_iota(jnp.int32, (per_tile, feat), 1)
    row = lax.broadcasted_iota(jnp.int32, (per_tile, feat), 0)
    own = row == lane // send_count
    index_rows = [halo[...]]
    for tile in range(partitions // per_tile):
        block = tiled[tile * per_tile : (tile + 1) * per_tile]
        index_rows.append(jnp.sum(jnp.where(own, block, 0), axis=0, keepdims=True))
    node_row = lax.broadcasted_iota(jnp.int32, (node_count, feat), 0)
    node_lane = lax.broadcasted_iota(jnp.int32, (feat, node_count), 1)
    ins[2].wait()
    feature_pair = beside(features[...])
    for at, index_row in enumerate(index_rows):
        listed = pl.ds(at * feat, feat)
        index_column = jnp.broadcast_to(index_row, (feat, feat)).T[:, :1]
        pick = jnp.where(index_column == node_lane, 1.0, 0.0).astype(BF16)
        outgoing[listed, :] = folded_columns(matmul(pick, feature_pair))
        placement[:, listed] = jnp.where(index_row == node_row, 1.0, 0.0).astype(BF16)

    pl.semaphore_wait(barrier, len(guests))

    def copy_to(source, target, sem, peer, group):
        return pltpu.make_async_remote_copy(
            src_ref=source,
            dst_ref=target,
            send_sem=send_sem.at[sem],
            recv_sem=recv_sem.at[sem],
            device_id=(peer, group),
            device_id_type=MESH,
        )

    def all_of(ref, sem):
        return copy_to(ref, ref, sem, dom, upper)

    def send_forward(sem, at):
        peer = dom_at(steps[at])
        copy_to(
            outgoing.at[pl.ds(halo_count + peer * send_count, send_count)],
            table.at[pl.ds(boundary + at * send_count, send_count)],
            sem,
            peer,
            grp,
        ).start()

    shared = outgoing.at[pl.ds(0, halo_count)]
    halo_up = copy_to(shared, table.at[pl.ds(0, halo_count)], 2, dom, upper)
    halo_down = copy_to(shared, table.at[pl.ds(halo_count, halo_count)], 3, dom, lower)
    for at in range(far_steps):
        send_forward(0, at)
    halo_up.start()
    halo_down.start()
    for at in range(far_steps, partitions - 1):
        send_forward(1, at)
    own_rows = pl.ds(boundary + (partitions - 1) * send_count, send_count)
    table[own_rows, :] = outgoing[pl.ds(halo_count + dom * send_count, send_count), :]

    ins[3].wait()
    ins[4].wait()
    slot = lax.broadcasted_iota(jnp.int32, (slot_count, node_count), 0)
    live = jnp.where(slot < degree[...], neighbours[...], -1)
    inverse_degree = 1.0 / degree[...].astype(F32)

    def count_rows(at, first):
        rows = first + lax.broadcasted_iota(jnp.int32, (send_count, node_count), 0)
        total = jnp.zeros((send_count, node_count), F32)
        for at_slot in range(slot_count):
            total = total + jnp.where(rows == live[at_slot : at_slot + 1], 1.0, 0.0)
        counts[pl.ds(at, send_count), :] = total.astype(BF16)

    def count_plain(step, carry):
        at = pl.multiple_of(step * send_count, send_count)
        count_rows(at, at)
        return carry

    lax.fori_loop(0, (node_count + boundary) // send_count, count_plain, 0)
    first = node_count + boundary
    for at, step in enumerate(steps + [(0, 0)]):
        count_rows(first + at * send_count, first + dom_before(step) * send_count)

    features_t = stacked(features[...].T)
    aggregate = folded_rows(matmul(features_t, counts[pl.ds(0, node_count), :]))
    for copy in ins[5:]:
        copy.wait()
    bias_column = jnp.broadcast_to(bias[...], (feat, feat)).T[:, :1]
    pre = folded_rows(matmul(weight_pair(w_self[...].T), features_t)) + bias_column
    neigh_t = weight_pair(w_neigh[...].T)
    neigh = weight_pair(w_neigh[...])
    cotangent_t = cotangent[...].T

    def taken(first, rows):
        return folded_rows(
            matmul(
                stacked(table[pl.ds(first, rows), :].T), counts[pl.ds(node_count + first, rows), :]
            )
        )

    halo_up.wait_recv()
    halo_down.wait_recv()
    sent_near = all_of(table.at[pl.ds(boundary + far_rows, near_rows)], 1)
    sent_near.wait_recv()
    aggregate = aggregate + taken(0, boundary)
    aggregate = aggregate + taken(boundary + far_rows, near_rows + send_count)
    sent_far = all_of(table.at[pl.ds(boundary, far_rows)], 0)
    sent_far.wait_recv()

    aggregate = aggregate + taken(boundary, far_rows)
    aggregate_t = stacked(aggregate * inverse_degree)
    pre = pre + folded_rows(matmul(neigh_t, aggregate_t))

    root = 0.7978845608028654
    square = pre * pre
    bent = jnp.tanh(root * (pre + 0.044715 * (square * pre)))
    rise = 0.5 * (1.0 + bent)
    slope = rise + 0.5 * pre * (1.0 - bent * bent) * (root * (1.0 + 3.0 * 0.044715 * square))
    pre_grad = stacked(cotangent_t * slope)

    product = folded_columns(
        matmul_nt(jnp.concatenate([features_t, aggregate_t], axis=0), pre_grad)
    )
    weight_grad[pl.ds(0, feat), :] = folded_rows(product[: 2 * feat])
    weight_grad[pl.ds(feat, feat), :] = folded_rows(product[2 * feat :])
    for peer, group, number in zx_peers:
        copy_to(
            weight_grad.at[pl.ds(number * piece_rows, piece_rows)],
            zx_slots.at[own_zx],
            7,
            peer,
            group,
        ).start()
    zx_slots[own_zx] = weight_grad[pl.ds(own_zx * piece_rows, piece_rows), :]
    ones = jnp.ones((16, node_count), BF16)
    x_bias[at_x] = folded_columns(matmul_nt(ones, pre_grad))[:1]
    for step in far_first(width_x)[:-1]:
        copy_to(x_bias.at[at_x], x_bias.at[at_x], 8, dom_at((0, step)), grp).start()

    edge_grad = stacked(folded_rows(matmul(neigh, pre_grad)) * inverse_degree)
    table_grad[...] = folded_columns(
        matmul_nt(counts[pl.ds(node_count, remote_rows), :], edge_grad)
    )

    def send_backward(at):
        copy_to(
            table_grad.at[pl.ds(boundary + at * send_count, send_count)],
            back.at[pl.ds(boundary + dom * send_count, send_count)],
            4,
            dom_before(steps[at]),
            grp,
        ).start()

    back_down = copy_to(
        table_grad.at[pl.ds(0, halo_count)], back.at[pl.ds(0, halo_count)], 5, dom, lower
    )
    back_up = copy_to(
        table_grad.at[pl.ds(halo_count, halo_count)],
        back.at[pl.ds(halo_count, halo_count)],
        6,
        dom,
        upper,
    )
    for at in range(partitions - 1):
        send_backward(at)
    back_down.start()
    back_up.start()
    back[pl.ds(boundary + dom * send_count, send_count), :] = table_grad[own_rows, :]

    activated[...] = (pre * rise).T
    own_grad = folded_columns(matmul_nt(counts[pl.ds(0, node_count), :], edge_grad))
    own_grad = own_grad + folded_rows(matmul(weight_pair(w_self[...]), pre_grad)).T

    def summed(slots):
        total = slots[0]
        for at in range(1, slots.shape[0]):
            total = total + slots[at]
        return total

    scattered = all_of(zx_slots.at[pl.ds(0, pieces - 1)], 7)
    scattered.wait_recv()
    yc_slots[own_yc] = summed(zx_slots)
    for peer, group in yc_peers:
        copy_to(yc_slots.at[own_yc], yc_slots.at[own_yc], 9, peer, group).start()
    bias_scattered = all_of(x_bias.at[pl.ds(0, width_x - 1)], 8)
    bias_scattered.wait_recv()
    yc_bias[own_yc] = summed(x_bias)
    for peer, group in yc_peers:
        copy_to(yc_bias.at[own_yc], yc_bias.at[own_yc], 10, peer, group).start()

    yc_sent = all_of(yc_slots.at[pl.ds(0, width_y * width_c - 1)], 9)
    yc_sent.wait_recv()
    own_part = pl.ds(own_zx * piece_rows, piece_rows)
    piece[...] = summed(yc_slots) * scale
    for peer, group, _ in zx_peers:
        copy_to(piece, gathered.at[own_part], 11, peer, group).start()
    gathered[own_part, :] = piece[...]
    yc_bias_sent = all_of(yc_bias.at[pl.ds(0, width_y * width_c - 1)], 10)
    yc_bias_sent.wait_recv()
    z_bias[at_z] = summed(yc_bias)
    for step in far_first(width_z)[:-1]:
        copy_to(z_bias.at[at_z], z_bias.at[at_z], 12, dom, grp_at(step, 0)).start()

    returned = all_of(back.at[pl.ds(0, (partitions - 1) * send_count)], 4)
    returned.wait_recv()
    back_down.wait_recv()
    back_up.wait_recv()
    extra = jnp.concatenate(
        [
            back[pl.ds(0, halo_count), :] + back[pl.ds(halo_count, halo_count), :],
            back[pl.ds(boundary, partitions * send_count), :],
        ],
        axis=0,
    )
    grad_features[...] = own_grad + folded_columns(matmul(placement[...], beside(extra)))
    z_bias_sent = all_of(z_bias.at[pl.ds(0, width_z - 1)], 12)
    z_bias_sent.wait_recv()
    total_b[...] = summed(z_bias) * scale
    collected = all_of(gathered.at[pl.ds(0, (pieces - 1) * piece_rows)], 11)
    collected.wait_recv()

    for copy in (
        sent_far,
        sent_near,
        halo_up,
        halo_down,
        returned,
        back_down,
        back_up,
        scattered,
        bias_scattered,
        yc_sent,
        yc_bias_sent,
        z_bias_sent,
        collected,
    ):
        copy.wait_send()


def put_out(activated, grad_features, gathered, total_b, *rest):
    *outs, out_sem = rest
    feat = gathered.shape[0] // 2
    sources = (
        activated,
        grad_features,
        gathered.at[pl.ds(0, feat)],
        gathered.at[pl.ds(feat, feat)],
        total_b,
    )
    copies = [
        pltpu.make_async_copy(source, target, out_sem.at[at])
        for at, (source, target) in enumerate(zip(sources, outs))
    ]
    for copy in copies:
        copy.start()
    for copy in copies:
        copy.wait()


def shards(features, w_self, w_neigh, bias, cotangent, neighbours, degree, halo_rows, send_rows):
    partitions = lax.axis_size("dom")
    groups = lax.axis_size("grp")
    node_count, feat = features.shape
    hidden = w_self.shape[1]
    halo_count = halo_rows.shape[0]
    send_count = send_rows.shape[3]
    slot_count = neighbours.shape[0]
    remote_rows = 2 * halo_count + partitions * send_count
    listed = halo_count + partitions * send_count
    width_y, width_z = partitions // WIDTH_X, groups // WIDTH_C
    widths = (width_y, WIDTH_X, width_z, WIDTH_C)
    pieces = width_z * WIDTH_X
    piece_rows = 2 * feat // pieces
    scale = 1.0 / (node_count * partitions * groups) ** 0.5
    outside = pl.BlockSpec(memory_space=pltpu.HBM)
    inside = pl.BlockSpec(memory_space=pltpu.VMEM)
    results = pl.pallas_call(
        functools.partial(kernel, widths, scale),
        out_shape=(
            pltpu.VMEM((node_count, hidden), F32),
            pltpu.VMEM((node_count, feat), F32),
            pltpu.VMEM((2 * feat, hidden), F32),
            pltpu.VMEM((1, hidden), F32),
        ),
        in_specs=[outside] * 9,
        out_specs=(inside,) * 4,
        scratch_shapes=[
            pltpu.VMEM((node_count, feat), F32),
            pltpu.VMEM((feat, hidden), F32),
            pltpu.VMEM((feat, hidden), F32),
            pltpu.VMEM((1, hidden), F32),
            pltpu.VMEM((node_count, hidden), F32),
            pltpu.VMEM((slot_count, node_count), jnp.int32),
            pltpu.VMEM((1, node_count), jnp.int32),
            pltpu.VMEM((1, halo_count), jnp.int32),
            pltpu.VMEM((send_count, partitions), jnp.int32),
            pltpu.VMEM((node_count + remote_rows, node_count), BF16),
            pltpu.VMEM((node_count, listed), BF16),
            pltpu.VMEM((listed, feat), F32),
            pltpu.VMEM((remote_rows, feat), F32),
            pltpu.VMEM((remote_rows, feat), F32),
            pltpu.VMEM((remote_rows, feat), F32),
            pltpu.VMEM((2 * feat, hidden), F32),
            pltpu.VMEM((pieces, piece_rows, hidden), F32),
            pltpu.VMEM((WIDTH_X, 1, hidden), F32),
            pltpu.VMEM((width_y * WIDTH_C, piece_rows, hidden), F32),
            pltpu.VMEM((width_y * WIDTH_C, 1, hidden), F32),
            pltpu.VMEM((width_z, 1, hidden), F32),
            pltpu.VMEM((piece_rows, hidden), F32),
            pltpu.SemaphoreType.DMA((9,)),
            pltpu.SemaphoreType.DMA((13,)),
            pltpu.SemaphoreType.DMA((13,)),
        ],
        compiler_params=pltpu.CompilerParams(
            collective_id=0, has_side_effects=True, vmem_limit_bytes=32 * 1024 * 1024
        ),
    )(
        *(
            pltpu.with_memory_space_constraint(value, pltpu.HBM)
            for value in (
                features,
                w_self,
                w_neigh,
                bias.reshape(1, hidden),
                cotangent,
                neighbours,
                degree.reshape(1, node_count),
                halo_rows.reshape(1, halo_count),
                jnp.swapaxes(send_rows, 2, 3).reshape(send_count, partitions),
            )
        )
    )
    activated, grad_features, grad_ws, grad_wn, grad_b = pl.pallas_call(
        put_out,
        out_shape=(
            jax.ShapeDtypeStruct((node_count, hidden), F32),
            jax.ShapeDtypeStruct((node_count, feat), F32),
            jax.ShapeDtypeStruct((feat, hidden), F32),
            jax.ShapeDtypeStruct((feat, hidden), F32),
            jax.ShapeDtypeStruct((1, hidden), F32),
        ),
        in_specs=[inside] * 4,
        out_specs=(outside,) * 5,
        scratch_shapes=[pltpu.SemaphoreType.DMA((5,))],
    )(*(pltpu.with_memory_space_constraint(value, pltpu.VMEM) for value in results))
    return activated, grad_features, grad_ws, grad_wn, grad_b.reshape(hidden)


def solution(mesh):
    placed = (
        P(("dom", "grp"), None),
        P(),
        P(),
        P(),
        P(("dom", "grp"), None),
        P(None, ("dom", "grp")),
        P(("dom", "grp")),
        P(("dom", "grp")),
        P("dom", "grp", None, None),
    )
    return jax.shard_map(
        shards,
        mesh=mesh,
        in_specs=placed,
        out_specs=(P(("dom", "grp"), None), P(("dom", "grp"), None), P(), P(), P()),
        check_vma=False,
    )
```

time: 59.5 us -> 45.3 us (0.76)
  local copies, waits for them, and re-layouts: 8.96 us -> 0 us
  Pallas kernels: 49.5 us -> 44.5 us
    unnamed x22 -> x0, local copies, waits for them, and re-layouts: 8.96 us -> none
    pallas_call x1 -> x2, Pallas kernels: 49.5 us -> 44.5 us  [the longest x1 43.7 us: shards(): pl.pallas_call(functools.partial(kernel, widths, scale), out_shape=(pltpu...]
where the time goes in v2:
time: 45.3 us; the launch traced here: 45.2 us
  Pallas kernels  44.5 us (98%)
  between operations  0.64 us (1%)
    pallas_call x1, Pallas kernels, shards(): pl.pallas_call(functools.partial(kernel, widths, scale), out_shape=(pltpu...  43.7 us

profile of v2, /device:TPU:1, one launch (start us, length us, event | category | flops | bytes accessed | tf_op | source)
XLA Modules:
  0.0 45.2 jit_solution(10909142247452753939)
XLA Ops:
  0.6 43.7 %shard_map.128 = (f32[512,128]{1,0:T(8,128)S(1)}, f32[512,128]{1,0:T(8,128)S(1)}, f32[256,128]{1,0:T(8,128)S(1)}, f32[1,128]{1,0:T(1,128)S(1)}) custom-call(f32[512,128]{1,0:T(8,128)} %features_hbm.1, f32[128,128]{1,0:T(8,128)} %w_self_hbm.1, f32[128,128]{1,0:T(8,128)} %w_neigh_hbm.1, f32[1,128]{1,0:T(1,128)} %bitcast.9, f32[512,128]{1,0:T(8,128)} %cotangent_hbm.1, ...), custom_call_target="tpu_custom_call" | custom-call | tf_op jit(solution)/shard_map/pallas_call | solution.py:462
  44.3 0.9 %shard_map.129 = (f32[512,128]{1,0:T(8,128)}, f32[512,128]{1,0:T(8,128)}, f32[128,128]{1,0:T(8,128)}, f32[128,128]{1,0:T(8,128)}, f32[1,128]{1,0:T(1,128)}) custom-call(f32[512,128]{1,0:T(8,128)S(1)} %get-tuple-element.14.activated, f32[512,128]{1,0:T(8,128)S(1)} %get-tuple-element.15.grad_features, f32[256,128]{1,0:T(8,128)S(1)} %get-tuple-element.16.gathered, ...), custom_call_target="tpu_custom_call" | custom-call | tf_op jit(solution)/shard_map/pallas_call | solution.py:518

commit v3 on v2

--- a/solution.py
+++ b/solution.py
@@ -53,8 +53,12 @@
     return lax.dot_general(left, right, (((1,), (1,)), ((), ())), preferred_element_type=F32)
 
 
+def apart(step, count):
+    return min(step, count - step)
+
+
 def far_first(count):
-    return sorted(range(count), key=lambda at: (-min(at, count - at), at))
+    return sorted(range(count), key=lambda at: -apart(at, count))
 
 
 def kernel(
@@ -89,12 +93,11 @@
     table_grad,
     back,
     weight_grad,
-    zx_slots,
-    x_bias,
-    yc_slots,
-    yc_bias,
+    sum_slots,
+    xc_bias,
+    across_slots,
+    y_bias,
     z_bias,
-    piece,
     in_sem,
     send_sem,
     recv_sem,
@@ -109,10 +112,10 @@
     remote_rows = table.shape[0]
     table_rows = node_count + remote_rows
     pieces = width_z * width_x
-    piece_rows = 2 * feat // pieces
+    piece_rows = feat // pieces
     boundary = 2 * halo_count
-    steps = [(step_y, step_x) for step_y in far_first(width_y) for step_x in far_first(width_x)]
-    steps.remove((0, 0))
+    steps = [(step_y, step_x) for step_y in range(width_y) for step_x in range(width_x)][1:]
+    steps.sort(key=lambda step: -apart(step[0], width_y) - apart(step[1], width_x))
     far_steps = partitions // 2
     far_rows = far_steps * send_count
     near_rows = (partitions - 1 - far_steps) * send_count
@@ -142,20 +145,21 @@
     def grp_at(step_z, step_c):
         return over_z[step_z] * width_c + over_c[step_c]
 
-    def apart(step, count):
-        return min(step, count - step)
-
-    zx_steps = [(step_z, step_x) for step_z in range(width_z) for step_x in range(width_x)][1:]
-    zx_steps.sort(key=lambda step: -apart(step[0], width_z) - apart(step[1], width_x))
-    zx_peers = [
-        (dom_at((0, step[1])), grp_at(step[0], 0), over_z[step[0]] * width_x + over_x[step[1]])
-        for step in zx_steps
+    first_core = at_c == 0
+    along, across = jnp.where(first_core, at_z, at_y), jnp.where(first_core, at_y, at_z)
+    own_number = along * width_x + at_x
+    own_piece = jnp.where(first_core, 0, pieces) + own_number
+    own_source = own_number * width_c + at_c
+    x_steps = [(step, step_x) for step in range(width_z) for step_x in range(width_x)][1:]
+    x_steps.sort(key=lambda step: -apart(step[0], width_z) - apart(step[1], width_x))
+    xc_peers = [
+        (dom_at((0, step_x)), grp_at(0, step_c))
+        for step_x in far_first(width_x)
+        for step_c in range(width_c)
+        if (step_x, step_c) != (0, 0)
     ]
-    own_zx = at_z * width_x + at_x
-    yc_steps = [(step_y, step_c) for step_y in far_first(width_y) for step_c in range(width_c)]
-    yc_steps.remove((0, 0))
-    yc_peers = [(dom_at((step[0], 0)), grp_at(0, step[1])) for step in yc_steps]
-    own_yc = at_y * width_c + at_c
+    y_peers = [(dom_at((step, 0)), grp) for step in far_first(width_y)[:-1]]
+    z_peers = [(dom, grp_at(step, 0)) for step in far_first(width_z)[:-1]]
 
     ins = [
         pltpu.make_async_copy(source, target, in_sem.at[at])
@@ -177,10 +181,11 @@
         copy.start()
 
     barrier = pltpu.get_barrier_semaphore()
-    guests = [(dom_at(step), grp) for step in steps]
-    guests += [peer[:2] for step, peer in zip(zx_steps, zx_peers) if step[0] != 0]
-    guests += [peer for step, peer in zip(yc_steps, yc_peers) if step[1] != 0]
-    guests += [(dom, upper), (dom, lower)]
+    offsets = [(step_y, step_x, 0, 0) for step_y, step_x in steps]
+    offsets += [(0, step_x, step, step_c) for step, step_x in x_steps for step_c in range(width_c) if step]
+    offsets += [(step_y, step_x, 0, 1) for step_y, step_x in steps + [(0, 0)]]
+    offsets.sort(key=lambda at: sum(map(apart, at, (width_y, width_x, width_z, width_c))), reverse=True)
+    guests = [(dom_at(at[:2]), grp_at(*at[2:])) for at in offsets]
     for guest in guests:
         pl.semaphore_signal(barrier, inc=1, device_id=guest, device_id_type=MESH)
 
@@ -285,14 +290,13 @@
 
     halo_up.wait_recv()
     halo_down.wait_recv()
+    aggregate = aggregate + taken(0, boundary)
+    sent_far = all_of(table.at[pl.ds(boundary, far_rows)], 0)
+    sent_far.wait_recv()
+    aggregate = aggregate + taken(boundary, far_rows)
     sent_near = all_of(table.at[pl.ds(boundary + far_rows, near_rows)], 1)
     sent_near.wait_recv()
-    aggregate = aggregate + taken(0, boundary)
     aggregate = aggregate + taken(boundary + far_rows, near_rows + send_count)
-    sent_far = all_of(table.at[pl.ds(boundary, far_rows)], 0)
-    sent_far.wait_recv()
-
-    aggregate = aggregate + taken(boundary, far_rows)
     aggregate_t = stacked(aggregate * inverse_degree)
     pre = pre + folded_rows(matmul(neigh_t, aggregate_t))
 
@@ -306,21 +310,40 @@
     product = folded_columns(
         matmul_nt(jnp.concatenate([features_t, aggregate_t], axis=0), pre_grad)
     )
-    weight_grad[pl.ds(0, feat), :] = folded_rows(product[: 2 * feat])
-    weight_grad[pl.ds(feat, feat), :] = folded_rows(product[2 * feat :])
-    for peer, group, number in zx_peers:
-        copy_to(
-            weight_grad.at[pl.ds(number * piece_rows, piece_rows)],
-            zx_slots.at[own_zx],
-            7,
-            peer,
-            group,
-        ).start()
-    zx_slots[own_zx] = weight_grad[pl.ds(own_zx * piece_rows, piece_rows), :]
+    for half in range(2):
+        part = folded_rows(product[2 * feat * half : 2 * feat * (half + 1)])
+        for at in range(pieces):
+            weight_grad[half * pieces + at] = part[at * piece_rows : (at + 1) * piece_rows]
+
+    def send_piece(number, source, peer, group):
+        copy_to(weight_grad.at[number], sum_slots.at[source], 7, peer, group).start()
+
+    for step, step_x in x_steps:
+        peer_x = over_x[step_x]
+        send_piece(
+            over_z[step] * width_x + peer_x,
+            (at_z * width_x + at_x) * width_c + at_c,
+            at_y * width_x + peer_x,
+            over_z[step] * width_c,
+        )
+        send_piece(
+            pieces + over_y[step] * width_x + peer_x,
+            (at_y * width_x + at_x) * width_c + at_c,
+            over_y[step] * width_x + peer_x,
+            at_z * width_c + 1,
+        )
+    send_piece(
+        jnp.where(first_core, pieces, 0) + across * width_x + at_x,
+        (across * width_x + at_x) * width_c + at_c,
+        dom,
+        grp_at(0, 1),
+    )
+    sum_slots[own_source] = weight_grad[own_piece]
     ones = jnp.ones((16, node_count), BF16)
-    x_bias[at_x] = folded_columns(matmul_nt(ones, pre_grad))[:1]
-    for step in far_first(width_x)[:-1]:
-        copy_to(x_bias.at[at_x], x_bias.at[at_x], 8, dom_at((0, step)), grp).start()
+    own_xc = at_x * width_c + at_c
+    xc_bias[own_xc] = folded_columns(matmul_nt(ones, pre_grad))[:1]
+    for peer, group in xc_peers:
+        copy_to(xc_bias.at[own_xc], xc_bias.at[own_xc], 8, peer, group).start()
 
     edge_grad = stacked(folded_rows(matmul(neigh, pre_grad)) * inverse_degree)
     table_grad[...] = folded_columns(
@@ -356,35 +379,50 @@
     own_grad = folded_columns(matmul_nt(counts[pl.ds(0, node_count), :], edge_grad))
     own_grad = own_grad + folded_rows(matmul(weight_pair(w_self[...]), pre_grad)).T
 
+    def in_order(own, at):
+        return lambda part: jnp.where(own <= at, part(at + 1), part(at))
+
+    line = []
+    for at in range(pieces * width_c - 1):
+        pick = in_order(own_source, at)
+        peer_a = pick(lambda place: place // (width_x * width_c))
+        peer_x = pick(lambda place: place // width_c % width_x)
+        peer_c = pick(lambda place: place % width_c)
+        peer_y, peer_z = jnp.where(first_core, at_y, peer_a), jnp.where(first_core, peer_a, at_z)
+        line.append((peer_y * width_x + peer_x, peer_z * width_c + peer_c))
+    across_line = []
+    for at in range(width_y - 1):
+        place = in_order(across, at)(lambda place: place)
+        peer_y, peer_z = jnp.where(first_core, place, at_y), jnp.where(first_core, at_z, place)
+        across_line.append((peer_y * width_x + at_x, peer_z * width_c + at_c))
+
     def summed(slots):
         total = slots[0]
         for at in range(1, slots.shape[0]):
             total = total + slots[at]
         return total
 
-    scattered = all_of(zx_slots.at[pl.ds(0, pieces - 1)], 7)
+    scattered = all_of(sum_slots.at[pl.ds(0, pieces * width_c - 1)], 7)
     scattered.wait_recv()
-    yc_slots[own_yc] = summed(zx_slots)
-    for peer, group in yc_peers:
-        copy_to(yc_slots.at[own_yc], yc_slots.at[own_yc], 9, peer, group).start()
-    bias_scattered = all_of(x_bias.at[pl.ds(0, width_x - 1)], 8)
+    across_slots[across] = summed(sum_slots)
+    for peer, group in across_line:
+        copy_to(across_slots.at[across], across_slots.at[across], 9, peer, group).start()
+    bias_scattered = all_of(xc_bias.at[pl.ds(0, width_x * width_c - 1)], 8)
     bias_scattered.wait_recv()
-    yc_bias[own_yc] = summed(x_bias)
-    for peer, group in yc_peers:
-        copy_to(yc_bias.at[own_yc], yc_bias.at[own_yc], 10, peer, group).start()
-
-    yc_sent = all_of(yc_slots.at[pl.ds(0, width_y * width_c - 1)], 9)
-    yc_sent.wait_recv()
-    own_part = pl.ds(own_zx * piece_rows, piece_rows)
-    piece[...] = summed(yc_slots) * scale
-    for peer, group, _ in zx_peers:
-        copy_to(piece, gathered.at[own_part], 11, peer, group).start()
-    gathered[own_part, :] = piece[...]
-    yc_bias_sent = all_of(yc_bias.at[pl.ds(0, width_y * width_c - 1)], 10)
-    yc_bias_sent.wait_recv()
-    z_bias[at_z] = summed(yc_bias)
-    for step in far_first(width_z)[:-1]:
-        copy_to(z_bias.at[at_z], z_bias.at[at_z], 12, dom, grp_at(step, 0)).start()
+    y_bias[at_y] = summed(xc_bias)
+    for peer, group in y_peers:
+        copy_to(y_bias.at[at_y], y_bias.at[at_y], 10, peer, group).start()
+
+    across_sent = all_of(across_slots.at[pl.ds(0, width_y - 1)], 9)
+    across_sent.wait_recv()
+    gathered[own_piece] = summed(across_slots) * scale
+    for peer, group in line:
+        copy_to(gathered.at[own_piece], gathered.at[own_piece], 11, peer, group).start()
+    y_bias_sent = all_of(y_bias.at[pl.ds(0, width_y - 1)], 10)
+    y_bias_sent.wait_recv()
+    z_bias[at_z] = summed(y_bias)
+    for peer, group in z_peers:
+        copy_to(z_bias.at[at_z], z_bias.at[at_z], 12, peer, group).start()
 
     returned = all_of(back.at[pl.ds(0, (partitions - 1) * send_count)], 4)
     returned.wait_recv()
@@ -401,7 +439,7 @@
     z_bias_sent = all_of(z_bias.at[pl.ds(0, width_z - 1)], 12)
     z_bias_sent.wait_recv()
     total_b[...] = summed(z_bias) * scale
-    collected = all_of(gathered.at[pl.ds(0, (pieces - 1) * piece_rows)], 11)
+    collected = all_of(gathered.at[pl.ds(0, 2 * pieces - 1)], 11)
     collected.wait_recv()
 
     for copy in (
@@ -414,8 +452,8 @@
         back_up,
         scattered,
         bias_scattered,
-        yc_sent,
-        yc_bias_sent,
+        across_sent,
+        y_bias_sent,
         z_bias_sent,
         collected,
     ):
@@ -423,21 +461,22 @@
 
 
 def put_out(activated, grad_features, gathered, total_b, *rest):
-    *outs, out_sem = rest
-    feat = gathered.shape[0] // 2
-    sources = (
-        activated,
-        grad_features,
-        gathered.at[pl.ds(0, feat)],
-        gathered.at[pl.ds(feat, feat)],
-        total_b,
-    )
+    *outs, grad_ws, grad_wn, out_sem = rest
+    pieces, piece_rows, _ = gathered.shape
+    pieces = pieces // 2
     copies = [
         pltpu.make_async_copy(source, target, out_sem.at[at])
-        for at, (source, target) in enumerate(zip(sources, outs))
+        for at, (source, target) in enumerate(
+            zip((activated, grad_features, grad_ws, grad_wn, total_b), outs)
+        )
     ]
-    for copy in copies:
-        copy.start()
+    copies[0].start()
+    copies[1].start()
+    copies[4].start()
+    for half, whole in enumerate((grad_ws, grad_wn)):
+        for at in range(pieces):
+            whole[pl.ds(at * piece_rows, piece_rows), :] = gathered[half * pieces + at]
+        copies[2 + half].start()
     for copy in copies:
         copy.wait()
 
@@ -455,7 +494,7 @@
     width_y, width_z = partitions // WIDTH_X, groups // WIDTH_C
     widths = (width_y, WIDTH_X, width_z, WIDTH_C)
     pieces = width_z * WIDTH_X
-    piece_rows = 2 * feat // pieces
+    piece_rows = feat // pieces
     scale = 1.0 / (node_count * partitions * groups) ** 0.5
     outside = pl.BlockSpec(memory_space=pltpu.HBM)
     inside = pl.BlockSpec(memory_space=pltpu.VMEM)
@@ -464,7 +503,7 @@
         out_shape=(
             pltpu.VMEM((node_count, hidden), F32),
             pltpu.VMEM((node_count, feat), F32),
-            pltpu.VMEM((2 * feat, hidden), F32),
+            pltpu.VMEM((2 * pieces, piece_rows, hidden), F32),
             pltpu.VMEM((1, hidden), F32),
         ),
         in_specs=[outside] * 9,
@@ -485,13 +524,12 @@
             pltpu.VMEM((remote_rows, feat), F32),
             pltpu.VMEM((remote_rows, feat), F32),
             pltpu.VMEM((remote_rows, feat), F32),
-            pltpu.VMEM((2 * feat, hidden), F32),
-            pltpu.VMEM((pieces, piece_rows, hidden), F32),
-            pltpu.VMEM((WIDTH_X, 1, hidden), F32),
-            pltpu.VMEM((width_y * WIDTH_C, piece_rows, hidden), F32),
-            pltpu.VMEM((width_y * WIDTH_C, 1, hidden), F32),
+            pltpu.VMEM((2 * pieces, piece_rows, hidden), F32),
+            pltpu.VMEM((pieces * WIDTH_C, piece_rows, hidden), F32),
+            pltpu.VMEM((WIDTH_X * WIDTH_C, 1, hidden), F32),
+            pltpu.VMEM((width_y, piece_rows, hidden), F32),
+            pltpu.VMEM((width_y, 1, hidden), F32),
             pltpu.VMEM((width_z, 1, hidden), F32),
-            pltpu.VMEM((piece_rows, hidden), F32),
             pltpu.SemaphoreType.DMA((9,)),
             pltpu.SemaphoreType.DMA((13,)),
             pltpu.SemaphoreType.DMA((13,)),
@@ -526,7 +564,11 @@
         ),
         in_specs=[inside] * 4,
         out_specs=(outside,) * 5,
-        scratch_shapes=[pltpu.SemaphoreType.DMA((5,))],
+        scratch_shapes=[
+            pltpu.VMEM((feat, hidden), F32),
+            pltpu.VMEM((feat, hidden), F32),
+            pltpu.SemaphoreType.DMA((5,)),
+        ],
     )(*(pltpu.with_memory_space_constraint(value, pltpu.VMEM) for value in results))
     return activated, grad_features, grad_ws, grad_wn, grad_b.reshape(hidden)
 

time: 45.3 us -> 44 us (0.971)
  Pallas kernels: 44.5 us -> 43.3 us
    pallas_call x1, Pallas kernels: 43.7 us -> 42.4 us  [shards(): pl.pallas_call(functools.partial(kernel, widths, scale), out_shape=(pltpu...]
where the time goes in v3:
time: 44 us; the launch traced here: 43.9 us
  Pallas kernels  43.3 us (98%)
  between operations  0.64 us (1%)
    pallas_call x1, Pallas kernels, shards(): pl.pallas_call(functools.partial(kernel, widths, scale), out_shape=(pltpu...  42.4 us

profile of v3, /device:TPU:1, one launch (start us, length us, event | category | flops | bytes accessed | tf_op | source)
XLA Modules:
  0.0 43.9 jit_solution(11009077839286004110)
XLA Ops:
  0.6 42.4 %shard_map.128 = (f32[512,128]{1,0:T(8,128)S(1)}, f32[512,128]{1,0:T(8,128)S(1)}, f32[64,4,128]{2,1,0:T(4,128)S(1)}, f32[1,128]{1,0:T(1,128)S(1)}) custom-call(f32[512,128]{1,0:T(8,128)} %features_hbm.1, f32[128,128]{1,0:T(8,128)} %w_self_hbm.1, f32[128,128]{1,0:T(8,128)} %w_neigh_hbm.1, f32[1,128]{1,0:T(1,128)} %bitcast.9, f32[512,128]{1,0:T(8,128)} %cotangent_hbm.1, ...), custom_call_target="tpu_custom_call" | custom-call | tf_op jit(solution)/shard_map/pallas_call | solution.py:501
  43.0 0.9 %shard_map.129 = (f32[512,128]{1,0:T(8,128)}, f32[512,128]{1,0:T(8,128)}, f32[128,128]{1,0:T(8,128)}, f32[128,128]{1,0:T(8,128)}, f32[1,128]{1,0:T(1,128)}) custom-call(f32[512,128]{1,0:T(8,128)S(1)} %get-tuple-element.14.activated, f32[512,128]{1,0:T(8,128)S(1)} %get-tuple-element.15.grad_features, f32[64,4,128]{2,1,0:T(4,128)S(1)} %get-tuple-element.16.gathered, ...), custom_call_target="tpu_custom_call" | custom-call | tf_op jit(solution)/shard_map/pallas_call | solution.py:556

commit v4 on v3

--- a/solution.py
+++ b/solution.py
@@ -296,20 +296,32 @@
     aggregate = aggregate + taken(boundary, far_rows)
     sent_near = all_of(table.at[pl.ds(boundary + far_rows, near_rows)], 1)
     sent_near.wait_recv()
-    aggregate = aggregate + taken(boundary + far_rows, near_rows + send_count)
-    aggregate_t = stacked(aggregate * inverse_degree)
-    pre = pre + folded_rows(matmul(neigh_t, aggregate_t))
-
+
+    first = boundary + far_rows
+    last_rows = near_rows + send_count
+    last_t = stacked(table[pl.ds(first, last_rows), :].T)
     root = 0.7978845608028654
-    square = pre * pre
-    bent = jnp.tanh(root * (pre + 0.044715 * (square * pre)))
-    rise = 0.5 * (1.0 + bent)
-    slope = rise + 0.5 * pre * (1.0 - bent * bent) * (root * (1.0 + 3.0 * 0.044715 * square))
-    pre_grad = stacked(cotangent_t * slope)
-
-    product = folded_columns(
-        matmul_nt(jnp.concatenate([features_t, aggregate_t], axis=0), pre_grad)
-    )
+    product = 0.0
+    pre_grads, active = [], []
+    for at in range(0, node_count, node_count // 2):
+        some = slice(at, at + node_count // 2)
+        last_counts = counts[pl.ds(node_count + first, last_rows), some]
+        sum_some = aggregate[:, some] + folded_rows(matmul(last_t, last_counts))
+        aggregate_t = stacked(sum_some * inverse_degree[:, some])
+        pre_some = pre[:, some] + folded_rows(matmul(neigh_t, aggregate_t))
+        square = pre_some * pre_some
+        bent = jnp.tanh(root * (pre_some + 0.044715 * (square * pre_some)))
+        rise = 0.5 * (1.0 + bent)
+        slope = rise + 0.5 * pre_some * (1.0 - bent * bent) * (
+            root * (1.0 + 3.0 * 0.044715 * square)
+        )
+        pre_grads.append(stacked(cotangent_t[:, some] * slope))
+        active.append(pre_some * rise)
+        both = jnp.concatenate([features_t[:, some], aggregate_t], axis=0)
+        product = product + matmul_nt(both, pre_grads[-1])
+    pre_grad = jnp.concatenate(pre_grads, axis=1)
+
+    product = folded_columns(product)
     for half in range(2):
         part = folded_rows(product[2 * feat * half : 2 * feat * (half + 1)])
         for at in range(pieces):
@@ -375,7 +387,7 @@
     back_up.start()
     back[pl.ds(boundary + dom * send_count, send_count), :] = table_grad[own_rows, :]
 
-    activated[...] = (pre * rise).T
+    activated[...] = jnp.concatenate(active, axis=1).T
     own_grad = folded_columns(matmul_nt(counts[pl.ds(0, node_count), :], edge_grad))
     own_grad = own_grad + folded_rows(matmul(weight_pair(w_self[...]), pre_grad)).T
 

time: 44 us -> 44 us (level)
  no operation moved by 1% of the time
where the time goes in v4:
time: 44 us; the launch traced here: 43.9 us
  Pallas kernels  43.3 us (98%)
  between operations  0.64 us (1%)
    pallas_call x1, Pallas kernels, shards(): pl.pallas_call(functools.partial(kernel, widths, scale), out_shape=(pltpu...  42.4 us

profile of v4, /device:TPU:1, one launch (start us, length us, event | category | flops | bytes accessed | tf_op | source)
XLA Modules:
  0.0 43.9 jit_solution(1373954879781484428)
XLA Ops:
  0.6 42.4 %shard_map.128 = (f32[512,128]{1,0:T(8,128)S(1)}, f32[512,128]{1,0:T(8,128)S(1)}, f32[64,4,128]{2,1,0:T(4,128)S(1)}, f32[1,128]{1,0:T(1,128)S(1)}) custom-call(f32[512,128]{1,0:T(8,128)} %features_hbm.1, f32[128,128]{1,0:T(8,128)} %w_self_hbm.1, f32[128,128]{1,0:T(8,128)} %w_neigh_hbm.1, f32[1,128]{1,0:T(1,128)} %bitcast.9, f32[512,128]{1,0:T(8,128)} %cotangent_hbm.1, ...), custom_call_target="tpu_custom_call" | custom-call | tf_op jit(solution)/shard_map/pallas_call | solution.py:513
  43.1 0.9 %shard_map.129 = (f32[512,128]{1,0:T(8,128)}, f32[512,128]{1,0:T(8,128)}, f32[128,128]{1,0:T(8,128)}, f32[128,128]{1,0:T(8,128)}, f32[1,128]{1,0:T(1,128)}) custom-call(f32[512,128]{1,0:T(8,128)S(1)} %get-tuple-element.14.activated, f32[512,128]{1,0:T(8,128)S(1)} %get-tuple-element.15.grad_features, f32[64,4,128]{2,1,0:T(4,128)S(1)} %get-tuple-element.16.gathered, ...), custom_call_target="tpu_custom_call" | custom-call | tf_op jit(solution)/shard_map/pallas_call | solution.py:568

commit v5 on v4

--- a/solution.py
+++ b/solution.py
@@ -358,9 +358,11 @@
         copy_to(xc_bias.at[own_xc], xc_bias.at[own_xc], 8, peer, group).start()
 
     edge_grad = stacked(folded_rows(matmul(neigh, pre_grad)) * inverse_degree)
-    table_grad[...] = folded_columns(
-        matmul_nt(counts[pl.ds(node_count, remote_rows), :], edge_grad)
-    )
+
+    def put_rows(first, rows):
+        table_grad[pl.ds(first, rows), :] = folded_columns(
+            matmul_nt(counts[pl.ds(node_count + first, rows), :], edge_grad)
+        )
 
     def send_backward(at):
         copy_to(
@@ -381,10 +383,12 @@
         dom,
         upper,
     )
-    for at in range(partitions - 1):
+    put_rows(boundary, far_rows)
+    for at in range(far_steps):
         send_backward(at)
-    back_down.start()
-    back_up.start()
+    put_rows(boundary + far_rows, near_rows + send_count)
+    for at in range(far_steps, partitions - 1):
+        send_backward(at)
     back[pl.ds(boundary + dom * send_count, send_count), :] = table_grad[own_rows, :]
 
     activated[...] = jnp.concatenate(active, axis=1).T
@@ -419,6 +423,9 @@
     across_slots[across] = summed(sum_slots)
     for peer, group in across_line:
         copy_to(across_slots.at[across], across_slots.at[across], 9, peer, group).start()
+    put_rows(0, boundary)
+    back_down.start()
+    back_up.start()
     bias_scattered = all_of(xc_bias.at[pl.ds(0, width_x * width_c - 1)], 8)
     bias_scattered.wait_recv()
     y_bias[at_y] = summed(xc_bias)

time: 44 us -> 43.9 us (level)
  no operation moved by 1% of the time
where the time goes in v5:
time: 43.9 us; the launch traced here: 43.8 us
  Pallas kernels  43.2 us (98%)
  between operations  0.64 us (1%)
    pallas_call x1, Pallas kernels, shards(): pl.pallas_call(functools.partial(kernel, widths, scale), out_shape=(pltpu...  42.3 us

profile of v5, /device:TPU:1, one launch (start us, length us, event | category | flops | bytes accessed | tf_op | source)
XLA Modules:
  0.0 43.8 jit_solution(10128861923577336105)
XLA Ops:
  0.6 42.3 %shard_map.128 = (f32[512,128]{1,0:T(8,128)S(1)}, f32[512,128]{1,0:T(8,128)S(1)}, f32[64,4,128]{2,1,0:T(4,128)S(1)}, f32[1,128]{1,0:T(1,128)S(1)}) custom-call(f32[512,128]{1,0:T(8,128)} %features_hbm.1, f32[128,128]{1,0:T(8,128)} %w_self_hbm.1, f32[128,128]{1,0:T(8,128)} %w_neigh_hbm.1, f32[1,128]{1,0:T(1,128)} %bitcast.9, f32[512,128]{1,0:T(8,128)} %cotangent_hbm.1, ...), custom_call_target="tpu_custom_call" | custom-call | tf_op jit(solution)/shard_map/pallas_call | solution.py:520
  42.9 0.9 %shard_map.129 = (f32[512,128]{1,0:T(8,128)}, f32[512,128]{1,0:T(8,128)}, f32[128,128]{1,0:T(8,128)}, f32[128,128]{1,0:T(8,128)}, f32[1,128]{1,0:T(1,128)}) custom-call(f32[512,128]{1,0:T(8,128)S(1)} %get-tuple-element.14.activated, f32[512,128]{1,0:T(8,128)S(1)} %get-tuple-element.15.grad_features, f32[64,4,128]{2,1,0:T(4,128)S(1)} %get-tuple-element.16.gathered, ...), custom_call_target="tpu_custom_call" | custom-call | tf_op jit(solution)/shard_map/pallas_call | solution.py:575
